TPU v7x, 768 devices: a whole 4x8x12 slice. The times are simulated.
768 devices in a mesh: dp: 32 (over y, z_lo), tensor: 24 (over x, z_hi, core).
Axes of the slice: x: 4, y: 8, z: 12 (z_hi: 3, z_lo: 4; z = z_hi * 4 + z_lo), core: 2. Of those that a mesh axis runs over, the one named last changes fastest.
Arguments:
- image_emb: float32 [196608, 1152], P(('dp', 'tensor')), may hold values from -6 to 6
- text_emb: float32 [196608, 1152], P(('dp', 'tensor')), may hold values from -6 to 6
- pooled: bfloat16 [196608, 1152], P(('dp', 'tensor')), may hold values from -1.25 to 1.25
- pairs: int32 [196608], P(('dp', 'tensor')), may hold values from 0 to 196607, as said below
- logit_scale: float32 [1], replicated, may hold values from 4 to 16
- logit_bias: float32 [1], replicated, may hold values from -3 to -1
Outputs:
- image_grad: float32 [196608, 1152], P(('dp', 'tensor'))
- weight_grad: float32 [1152, 1152], P('tensor')
Inputs may be any that keep to these rules, and one draw needn't show every extreme that they name: pairs[i] lies in the window of row i; several images may share a positive text.
All inputs are finite; a program needn't handle non-finite values.
Results may differ from a plain program's by a relative error of at most 0.0052.
Values may be sent and summed in bfloat16 or wider, within the bound.
A program may use at most 32 MiB of HBM per device.

v0:
```python
import jax
import jax.numpy as jnp
from jax import lax
from jax.sharding import PartitionSpec as P


def from_behind(block, axis, distance):
    devices = range(lax.axis_size(axis))
    route = [((i - distance) % len(devices), i) for i in devices]
    return lax.ppermute(block, axis, route)


def on_device(image_emb, text_emb, pooled, pairs, logit_scale, logit_bias):
    rows = image_emb.shape[0]
    width = image_emb.shape[1]
    n_data = lax.axis_size("dp")
    n_group = lax.axis_size("tensor")
    inv_img = lax.rsqrt(jnp.sum(image_emb * image_emb, axis=1, keepdims=True) + 1e-06)
    unit = image_emb * inv_img
    unit_copy = unit.astype(jnp.bfloat16)
    text_copy = (
        text_emb * lax.rsqrt(jnp.sum(text_emb * text_emb, axis=1, keepdims=True) + 1e-06)
    ).astype(jnp.bfloat16)
    behind = from_behind(text_copy, "dp", 1)
    ahead = []
    current = text_copy
    for hop in range(2):
        current = from_behind(current, "dp", -1)
        ahead.append(current)
    near, far = (ahead[0], ahead[1])
    blocks = [behind, text_copy, near, far]
    scale = logit_scale[0]
    bias = logit_bias[0]
    logits = (
        jnp.concatenate(
            [
                lax.dot_general(
                    unit_copy, block, (((1,), (1,)), ((), ())), preferred_element_type=jnp.float32
                )
                for block in blocks
            ],
            axis=1,
        )
        * scale
        + bias
    )
    group = lax.axis_index("dp")
    owner = pairs // rows // n_group
    column = (owner - group + 1 + n_data) % n_data * rows + pairs % rows
    positions = lax.broadcasted_iota(jnp.int32, (1, 4 * rows), 1)
    labels = (positions == column[:, None]).astype(jnp.float32)
    coeff = (jax.nn.sigmoid(logits) - labels).astype(jnp.bfloat16)
    grad_unit = jnp.zeros((rows, width), jnp.float32)
    for place, block in enumerate(blocks):
        part_coeff = coeff[:, place * rows : (place + 1) * rows]
        grad_unit = grad_unit + jnp.dot(part_coeff, block, preferred_element_type=jnp.float32)
    grad_unit = scale * grad_unit
    image_grad = inv_img * (grad_unit - unit * jnp.sum(unit * grad_unit, axis=1, keepdims=True))
    cached = image_grad.astype(jnp.bfloat16)
    own_rows = lax.psum_scatter(
        lax.dot_general(
            pooled, cached, (((0,), (0,)), ((), ())), preferred_element_type=jnp.float32
        ),
        "tensor",
        scatter_dimension=0,
        tiled=True,
    )
    weight_grad = lax.psum(own_rows, "dp")
    return (image_grad, weight_grad)


def solution(mesh):
    in_specs = (
        P(("dp", "tensor"), None),
        P(("dp", "tensor"), None),
        P(("dp", "tensor"), None),
        P(("dp", "tensor")),
        P(),
        P(),
    )
    out_specs = (P(("dp", "tensor"), None), P("tensor", None))
    return jax.shard_map(
        on_device, mesh=mesh, in_specs=in_specs, out_specs=out_specs, check_vma=False
    )
```

profile of v0, /device:TPU:6, one launch (start us, length us, event | category | flops | bytes accessed | tf_op | source)
XLA Modules:
  0.0 550.5 jit_solution(6372278767032818622)
XLA Ops:
  7.2 0.0 copy-start
  7.2 0.0 reduce-scatter.4.cloned.1.call-start
  7.2 1.5 multiply_reduce_fusion.1
  8.8 0.1 copy-done.3
  8.9 0.1 multiply_convert_fusion
  9.0 10.9 %collective-permute-start.1 = (bf16[256,1152]{1,0:T(8,128)(2,1)S(1)}, bf16[256,1152]{1,0:T(8,128)(2,1)S(1)}, u32[]{:S(2)}, u32[]{:S(2)}) collective-permute-start(bf16[256,1152]{1,0:T(8,128)(2,1)S(1)} %multiply_convert_fusion), channel_id=1, source_target_pairs={{24,0},{48,24},{72,48},{96,72},{120,96},{144,120},{168,144},{192,1... | collective-permute-start | bytes 1769480 | tf_op jit(solution)/shard_map/ppermute | solution.py:10
  20.0 1.9 collective-permute-start
  21.9 0.2 multiply_reduce_fusion.2
  22.1 0.1 multiply_convert_fusion.1
  22.2 1.1 fusion.20
  23.3 10.4 %collective-permute-done.1 = bf16[256,1152]{1,0:T(8,128)(2,1)S(1)} collective-permute-done((bf16[256,1152]{1,0:T(8,128)(2,1)S(1)}, bf16[256,1152]{1,0:T(8,128)(2,1)S(1)}, u32[]{:S(2)}, u32[]{:S(2)}) %collective-permute-start.1) | collective-permute-done | bytes 589856 | tf_op jit(solution)/shard_map/ppermute | solution.py:10
  33.7 8.3 %collective-permute-start.2 = (bf16[256,1152]{1,0:T(8,128)(2,1)S(1)}, bf16[256,1152]{1,0:T(8,128)(2,1)S(1)}, u32[]{:S(2)}, u32[]{:S(2)}) collective-permute-start(bf16[256,1152]{1,0:T(8,128)(2,1)S(1)} %collective-permute-done.1), channel_id=1, source_target_pairs={{24,0},{48,24},{72,48},{96,72},{120,96},{144,120},{168,144},{192,1... | collective-permute-start | bytes 1769480 | tf_op jit(solution)/shard_map/ppermute | solution.py:10
  43.3 0.4 fusion.21
  43.7 3.2 collective-permute-done
  46.9 1.4 fusion.19
  48.4 9.5 %collective-permute-done.2 = bf16[256,1152]{1,0:T(8,128)(2,1)S(1)} collective-permute-done((bf16[256,1152]{1,0:T(8,128)(2,1)S(1)}, bf16[256,1152]{1,0:T(8,128)(2,1)S(1)}, u32[]{:S(2)}, u32[]{:S(2)}) %collective-permute-start.2) | collective-permute-done | bytes 589856 | tf_op jit(solution)/shard_map/ppermute | solution.py:10
  57.9 0.4 fusion.22
  58.3 0.4 fusion.8
  58.6 0.4 fusion.13
  59.0 0.4 fusion.11
  59.4 1.5 fusion
  60.9 0.5 multiply_reduce_fusion
  61.3 0.3 subtract_multiply_fusion
  61.6 3.3 convolution_bitcast_fusion
  65.0 6.9 %copy.10 = f32[1152,1152]{1,0:T(8,128)} copy(f32[1152,1152]{0,1:T(8,128)} %convolution_bitcast_fusion) | data formatting | bytes 10616832
  71.9 0.0 reduce-scatter.4.cloned.1.call-update
  71.9 0.0 all-reduce.2.cloned.1.call-start
  71.9 163.9 %reduce-scatter.4.cloned.1.call-done = f32[48,1152]{1,0:T(8,128)} async-done(((f32[1152,1152]{1,0:T(8,128)}), f32[48,1152]{1,0:T(8,128)}) %reduce-scatter.4.cloned.1.call-update) | async-done | bytes 221200
  235.8 2.0 copy.11
  237.8 0.0 all-reduce.2.cloned.1.call-update
  237.8 303.9 %all-reduce.2.cloned.1.call-done = f32[48,1152]{0,1:T(8,128)} async-done(((f32[48,1152]{0,1:T(8,128)}), f32[48,1152]{0,1:T(8,128)}) %all-reduce.2.cloned.1.call-update) | async-done | bytes 221200 | tf_op jit(solution)/shard_map/psum | solution.py:68
  541.7 2.0 copy.9
  (13 shorter events, 0.1 us)
Async XLA Ops:
  7.2 54.5 %copy-start = (bf16[256,1152]{1,0:T(8,128)(2,1)S(1)}, bf16[256,1152]{1,0:T(8,128)(2,1)}, u32[]{:S(2)}) copy-start(bf16[256,1152]{1,0:T(8,128)(2,1)} %param.8) | copy-start | bytes 1769476
  7.2 228.6 %reduce-scatter.4.cloned.1.call-start = ((), (), s32[]{:S(2)}) async-start(), calls=%async_computation.2 | async-start | bytes 5529600
  7.2 1.7 copy-start.3
  8.8 13.1 %copy-start.1 = (f32[256,1152]{1,0:T(8,128)S(1)}, f32[256,1152]{1,0:T(8,128)}, u32[]{:S(2)}) copy-start(f32[256,1152]{1,0:T(8,128)} %param.6) | copy-start | bytes 3538948
  9.0 24.7 %collective-permute-start.1 = (bf16[256,1152]{1,0:T(8,128)(2,1)S(1)}, bf16[256,1152]{1,0:T(8,128)(2,1)S(1)}, u32[]{:S(2)}, u32[]{:S(2)}) collective-permute-start(bf16[256,1152]{1,0:T(8,128)(2,1)S(1)} %multiply_convert_fusion), channel_id=1, source_target_pairs={{24,0},{48,24},{72,48},{96,72},{120,96},{144,120},{168,144},{192,1... | collective-permute-start | bytes 1769480 | tf_op jit(solution)/shard_map/ppermute | solution.py:10
  20.0 27.0 %collective-permute-start = (bf16[256,1152]{1,0:T(8,128)(2,1)S(1)}, bf16[256,1152]{1,0:T(8,128)(2,1)}, u32[]{:S(2)}, u32[]{:S(2)}) collective-permute-start(bf16[256,1152]{1,0:T(8,128)(2,1)S(1)} %multiply_convert_fusion), channel_id=1, source_target_pairs={{744,0},{0,24},{24,48},{48,72},{72,96},{96,120},{120,144},{144,168... | collective-permute-start | bytes 1769480 | tf_op jit(solution)/shard_map/ppermute | solution.py:10
  22.1 19.9 %copy-start.5 = (s32[256]{0:T(256)S(1)}, s32[256]{0:T(256)}, u32[]{:S(2)}) copy-start(s32[256]{0:T(256)} %param.9) | copy-start | bytes 3076
  33.7 24.2 %collective-permute-start.2 = (bf16[256,1152]{1,0:T(8,128)(2,1)S(1)}, bf16[256,1152]{1,0:T(8,128)(2,1)S(1)}, u32[]{:S(2)}, u32[]{:S(2)}) collective-permute-start(bf16[256,1152]{1,0:T(8,128)(2,1)S(1)} %collective-permute-done.1), channel_id=1, source_target_pairs={{24,0},{48,24},{72,48},{96,72},{120,96},{144,120},{168,144},{192,1... | collective-permute-start | bytes 1769480 | tf_op jit(solution)/shard_map/ppermute | solution.py:10
  43.7 14.5 %copy-start.4 = (f32[256,256]{0,1:T(8,128)S(1)}, f32[256,256]{0,1:T(8,128)}, u32[]{:S(2)}) copy-start(f32[256,256]{0,1:T(8,128)} %fusion.20) | copy-start | bytes 786436
  61.6 3.4 copy-start.2
  71.9 469.8 %all-reduce.2.cloned.1.call-start = ((), (), s32[]{:S(2)}) async-start(), calls=%async_computation.1 | async-start | bytes 1179648 | tf_op jit(solution)/shard_map/psum | solution.py:68
Sparse Core Ops, SparseCore 0:
  72.0 163.7 reduce-scatter.3
  239.0 302.6 all-reduce.1
where the time goes:
time: 551 us; the launch traced here: 550 us
  waiting for transfers between devices  491 us (89%)
  starting transfers between devices  21.2 us (4%)
  between operations  15.5 us (3%)
  local copies, waits for them, and re-layouts  10.9 us (2%)
  matrix products  9.26 us (2%)
    psum x1, waiting for transfers between devices, on_device(): weight_grad = lax.psum(own_rows, 'dp')  304 us
    unnamed x3, waiting for transfers between devices  164 us
    ppermute x3, waiting for transfers between devices, from_behind(): return lax.ppermute(block, axis, route)  23.1 us
    ppermute x3, starting transfers between devices, from_behind(): return lax.ppermute(block, axis, route)  21.1 us
  transfers between devices with their start and end apart: 5, of which 5 were waited for; matrix products, arithmetic and copies ran while one was open for 1% of the time, Pallas kernels for 0%

commit v1 on v0

v1 whole, which is shorter than its diff:
```python
import functools

import jax
import jax.numpy as jnp
from jax import lax
from jax.experimental import pallas as pl
from jax.experimental.pallas import tpu as pltpu
from jax.sharding import PartitionSpec as P

X, ZH, Y, ZL = 4, 3, 8, 4
Z = ZH * ZL
H = 2
MESH = pl.DeviceIdType.MESH
BF16 = jnp.bfloat16
F32 = jnp.float32
TILE = (16, 128)


def kernel(
    image_hbm, text_hbm, pooled_hbm, column, scale_ref, bias_ref,
    grad_hbm, weight_out,
    image, text, pooled, unit, own, recv, total, grad, cached, cached_s,
    pt, pt_s, far_b, next_b, prev_b, next_f, prev_f,
    r1p, r1m, r2p, r2m, r3p, r3m,
    sum_f, sum_b, ry, vf, vb, rz, gathered,
    load_sem, t_send, t_recv, f_send, f_recv, x_send, x_recv,
    y_send, y_recv, z_send, z_recv, a_send, a_recv, b_send, b_recv,
):
    rows, width = image.shape
    step = rows // H
    cols = width // 128
    slab = width // (X * ZH * 2)
    ca = (cols + 1) // 2
    cb = cols - ca
    tall = slab // 16
    tiles = cols * tall

    dp = lax.axis_index("dp")
    t = lax.axis_index("tensor")
    y, p = dp // ZL, dp % ZL
    core = t % 2
    zh = (t // 2) % ZH
    x = t // (2 * ZH)
    z = zh * ZL + p

    def at(x_, y_, zh_, p_, core_):
        return (y_ * ZL + p_, (x_ * ZH + zh_) * 2 + core_)

    def z_dev(z_):
        return at(x, y, z_ // ZL, z_ % ZL, core)

    sibling = at(x, y, zh, p, 1 - core)
    x_next = at((x + 1) % X, y, zh, p, core)
    x_prev = at((x + X - 1) % X, y, zh, p, core)

    def remote(src, dst, send, recv_, device):
        return pltpu.make_async_remote_copy(
            src_ref=src, dst_ref=dst, send_sem=send, recv_sem=recv_,
            device_id=device, device_id_type=MESH,
        )

    load_text = pltpu.make_async_copy(text_hbm, text, load_sem.at[0])
    load_image = pltpu.make_async_copy(image_hbm, image, load_sem.at[1])
    load_pooled = pltpu.make_async_copy(pooled_hbm, pooled, load_sem.at[2])
    load_text.start()
    load_image.start()
    load_pooled.start()

    barrier = pltpu.get_barrier_semaphore()

    def greet(device):
        pl.semaphore_signal(barrier, inc=1, device_id=device, device_id_type=MESH)

    greet(at(x, (y + 1) % Y, zh, (p + ZL - 1) % ZL, core))
    greet(at(x, (y + Y - 1) % Y, zh, (p + 1) % ZL, core))
    greet(sibling)
    greet(x_next)
    greet(x_prev)

    @pl.loop(1, Y)
    def _(d):
        greet(at(x, (y + d) % Y, zh, p, core))

    @pl.loop(1, Z)
    def _(d):
        greet(z_dev((z + d) % Z))

    load_text.wait()
    for h in range(H):
        part = text[pl.ds(h * step, step), :]
        size = jnp.sum(part * part, axis=1, keepdims=True)
        own[h] = (part * lax.rsqrt(size + 1e-06)).astype(BF16)
    pl.semaphore_wait(barrier, 5 + (Y - 1) + (Z - 1))

    inner = jnp.logical_and(p >= 1, p <= 2)
    q_in = p - 1
    q_out = p // 3

    def text_copy(src, slot, h, send, y_, p_):
        return remote(
            src, recv.at[slot, h], t_send.at[send, h], t_recv.at[slot, h],
            at(x, y_, zh, p_, core),
        )

    def from_inner(which, h):
        q = q_in
        if which == 0:
            return text_copy(own.at[h], 1 - q, h, 0, y, 3 * q)
        if which == 1:
            return text_copy(own.at[h], q, h, 1, y, 2 - q)
        if which == 2:
            return text_copy(recv.at[1, h], 2, h, 2, y, q)
        if which == 3:
            return text_copy(recv.at[2, h], q, h, 3, (y + 1 - q) % Y, 3 * q)
        return text_copy(recv.at[0, h], 2, h, 4, (y + Y - 1) % Y, 2 + q)

    def from_outer(h):
        return text_copy(own.at[h], q_out, h, 0, y, 1 + q_out)

    @pl.when(inner)
    def _():
        for h in range(H):
            from_inner(0, h).start()
            from_inner(1, h).start()

    @pl.when(jnp.logical_not(inner))
    def _():
        for h in range(H):
            from_outer(h).start()

    load_pooled.wait()
    pt[...] = pooled[...].T.reshape(X * ZH, 2, slab, rows)
    pt_copy = remote(pt.at[:, 1 - core], pt_s, f_send.at[0], f_recv.at[0], sibling)
    pt_copy.start()

    scale = scale_ref[0]
    bias = bias_ref[0]
    load_image.wait()
    value = image[...]
    inv = lax.rsqrt(jnp.sum(value * value, axis=1, keepdims=True) + 1e-06)
    unit[...] = (value * inv).astype(BF16)
    sum_b[:, pl.ds(tiles, Y * ZL - tiles)] = jnp.zeros((ZH, Y * ZL - tiles, *TILE), BF16)

    def work(block, place, h):
        logits = lax.dot_general(
            unit[...], block, (((1,), (1,)), ((), ())), preferred_element_type=F32
        )
        logits = logits * scale + bias
        spot = lax.broadcasted_iota(jnp.int32, (rows, step), 1) + (place * rows + h * step)
        label = (spot == column[...]).astype(F32)
        coeff = (jax.nn.sigmoid(logits) - label).astype(BF16)
        return jnp.dot(coeff, block, preferred_element_type=F32)

    total[...] = work(own[0], 1, 0)
    for h in range(1, H):
        total[...] += work(own[h], 1, h)

    def arrive(slot, h):
        text_copy(recv.at[slot, h], slot, h, 0, y, p).wait_recv()

    first = jnp.where(p == 0, 1, 0)
    second = jnp.where(inner, 1, 2)
    third = jnp.where(p == 0, 0, jnp.where(p == 3, 1, 2))

    def take(slot, h, relay):
        arrive(slot, h)

        @pl.when(inner)
        def _():
            from_inner(relay, h).start()

        place = slot + jnp.minimum(slot, 1)
        total[...] += work(recv[slot, h], place, h)

    for h in range(H):
        take(first, h, 4)
        take(second, h, 2)
    for h in range(H):
        take(third, h, 3)

    def cached_copy(h):
        return remote(cached.at[h], cached_s.at[h], f_send.at[1 + h], f_recv.at[1 + h], sibling)

    def grad_copy(h):
        part = pl.ds(h * step, step)
        return pltpu.make_async_copy(grad.at[part], grad_hbm.at[part], load_sem.at[h])

    for h in range(H):
        part = pl.ds(h * step, step)
        value = image[part, :]
        inv = lax.rsqrt(jnp.sum(value * value, axis=1, keepdims=True) + 1e-06)
        line = value * inv
        full = scale * total[part, :]
        result = inv * (full - line * jnp.sum(line * full, axis=1, keepdims=True))
        grad[part, :] = result
        cached[h] = result.astype(BF16)
        cached_copy(h).start()
        grad_copy(h).start()

    pt_copy.wait_recv()
    for h in range(H):
        cached_copy(h).wait_recv()

    def product(x_):
        mine = pt[pl.ds(x_ * ZH, ZH), core].reshape(ZH * slab, rows)
        other = pt_s[pl.ds(x_ * ZH, ZH)].reshape(ZH * slab, rows)
        return jnp.dot(
            mine, cached[...].reshape(rows, width), preferred_element_type=F32
        ) + jnp.dot(other, cached_s[...].reshape(rows, width), preferred_element_type=F32)

    def block_of(value, c):
        return value[:, c * 128 : (c + 1) * 128].reshape(ZH, tall, *TILE)

    def x_copy(which, k):
        def go(src, dst, device):
            return remote(src, dst, x_send.at[which, k], x_recv.at[which, k], device)

        if which == 0:
            return go(far_b.at[k, pl.ds(0, ca)], r1p.at[k], x_next)
        if which == 1:
            return go(far_b.at[k, pl.ds(ca, cb)], r1m.at[k], x_prev)
        if which == 2:
            return go(next_b.at[k, pl.ds(ca, cb)], r2p.at[k], x_next)
        if which == 3:
            return go(prev_b.at[k, pl.ds(0, ca)], r2m.at[k], x_prev)
        if which == 4:
            return go(next_b.at[k, pl.ds(0, ca)], r3p.at[k], x_next)
        return go(prev_b.at[k, pl.ds(ca, cb)], r3m.at[k], x_prev)

    value = product((x + 2) % X)
    for c in range(cols):
        far_b[:, c] = block_of(value, c).astype(BF16)
    for k in range(ZH):
        x_copy(0, k).start()
        x_copy(1, k).start()
    value = product((x + 1) % X)
    for c in range(cols):
        if c < ca:
            next_f[:, c] = block_of(value, c)
        else:
            next_b[:, c] = block_of(value, c).astype(BF16)
    for k in range(ZH):
        x_copy(2, k).start()
    value = product((x + X - 1) % X)
    for c in range(cols):
        if c < ca:
            prev_b[:, c] = block_of(value, c).astype(BF16)
        else:
            prev_f[:, c - ca] = block_of(value, c)
    for k in range(ZH):
        x_copy(3, k).start()
    for k in range(ZH):
        x_copy(0, k).wait_recv()
        next_b[k, pl.ds(0, ca)] = (next_f[k] + r1p[k].astype(F32)).astype(BF16)
        x_copy(4, k).start()
        x_copy(1, k).wait_recv()
        prev_b[k, pl.ds(ca, cb)] = (prev_f[k] + r1m[k].astype(F32)).astype(BF16)
        x_copy(5, k).start()
    value = product(x)
    for c in range(cols):
        sum_f[:, pl.ds(c * tall, tall)] = block_of(value, c)

    def y_copy(k, d):
        to = (y + d) % Y
        return remote(
            sum_b.at[k, pl.ds(to * ZL, ZL)], ry.at[k, d - 1], y_send.at[k, d - 1],
            y_recv.at[k, d - 1], at(x, to, zh, p, core),
        )

    for k in range(ZH):
        x_copy(2, k).wait_recv()
        x_copy(3, k).wait_recv()
        x_copy(4, k).wait_recv()
        x_copy(5, k).wait_recv()
        low, high = pl.ds(0, ca * tall), pl.ds(ca * tall, cb * tall)
        left = r2m[k].astype(F32) + r3p[k].astype(F32)
        right = r2p[k].astype(F32) + r3m[k].astype(F32)
        value = sum_f[k, low] + left.reshape(ca * tall, *TILE)
        sum_f[k, low] = value
        sum_b[k, low] = value.astype(BF16)
        value = sum_f[k, high] + right.reshape(cb * tall, *TILE)
        sum_f[k, high] = value
        sum_b[k, high] = value.astype(BF16)

        @pl.loop(1, Y)
        def _(d):
            y_copy(k, d).start()

    for k in range(ZH):
        @pl.loop(1, Y)
        def _(d):
            y_copy(k, d).wait_recv()

        value = sum_f[k, pl.ds(y * ZL, ZL)]
        for d in range(Y - 1):
            value += ry[k, d].astype(F32)
        vf[pl.ds(k * ZL, ZL)] = value
        vb[pl.ds(k * ZL, ZL)] = value.astype(BF16)

    def z_copy(d):
        to = (z + d) % Z
        return remote(
            vb.at[to], rz.at[d - 1], z_send.at[d - 1], z_recv.at[d - 1], z_dev(to)
        )

    @pl.loop(1, Z)
    def _(d):
        z_copy(d).start()

    @pl.loop(1, Z)
    def _(d):
        z_copy(d).wait_recv()

    value = vf[z]
    for d in range(Z - 1):
        value += rz[d].astype(F32)
    gathered[y * ZL + p] = value.astype(BF16)

    def a_copy(d):
        mine = gathered.at[y * ZL + p]
        return remote(
            mine, mine, a_send.at[d - 1], a_recv.at[d - 1], at(x, y, zh, (p + d) % ZL, core)
        )

    def a_arrival(d):
        place = gathered.at[y * ZL + (p + ZL - d) % ZL]
        return remote(place, place, a_send.at[d - 1], a_recv.at[d - 1], sibling)

    def b_copy(d):
        mine = gathered.at[pl.ds(y * ZL, ZL)]
        return remote(
            mine, mine, b_send.at[d - 1], b_recv.at[d - 1], at(x, (y + d) % Y, zh, p, core)
        )

    def b_arrival(d):
        place = gathered.at[pl.ds((y + Y - d) % Y * ZL, ZL)]
        return remote(place, place, b_send.at[d - 1], b_recv.at[d - 1], sibling)

    @pl.loop(1, ZL)
    def _(d):
        a_copy(d).start()

    @pl.loop(1, ZL)
    def _(d):
        a_arrival(d).wait_recv()

    @pl.loop(1, Y)
    def _(d):
        b_copy(d).start()

    @pl.loop(1, Y)
    def _(d):
        b_arrival(d).wait_recv()

    for c in range(cols):
        for r in range(tall):
            weight_out[pl.ds(16 * r, 16), pl.ds(128 * c, 128)] = gathered[c * tall + r].astype(F32)

    @pl.when(inner)
    def _():
        for h in range(H):
            for which in range(5):
                from_inner(which, h).wait_send()

    @pl.when(jnp.logical_not(inner))
    def _():
        for h in range(H):
            from_outer(h).wait_send()

    pt_copy.wait_send()
    for h in range(H):
        cached_copy(h).wait_send()
        grad_copy(h).wait()
    for k in range(ZH):
        for which in range(6):
            x_copy(which, k).wait_send()

        @pl.loop(1, Y)
        def _(d):
            y_copy(k, d).wait_send()

    @pl.loop(1, Z)
    def _(d):
        z_copy(d).wait_send()

    @pl.loop(1, ZL)
    def _(d):
        a_copy(d).wait_send()

    @pl.loop(1, Y)
    def _(d):
        b_copy(d).wait_send()


def on_device(image_emb, text_emb, pooled, pairs, logit_scale, logit_bias):
    rows, width = image_emb.shape
    n_data = lax.axis_size("dp")
    n_group = lax.axis_size("tensor")
    slab = width // n_group
    step = rows // H
    cols = width // 128
    tall = slab // 16
    ca = (cols + 1) // 2
    cb = cols - ca
    owner = pairs // rows // n_group
    column = (owner - lax.axis_index("dp") + 1 + n_data) % n_data * rows + pairs % rows
    vmem = pltpu.VMEM
    dma = pltpu.SemaphoreType.DMA
    anywhere = pl.BlockSpec(memory_space=pl.ANY)
    in_vmem = pl.BlockSpec(memory_space=pltpu.VMEM)
    in_smem = pl.BlockSpec(memory_space=pltpu.SMEM)
    return pl.pallas_call(
        kernel,
        out_shape=(
            jax.ShapeDtypeStruct((rows, width), F32),
            jax.ShapeDtypeStruct((slab, width), F32),
        ),
        in_specs=[anywhere, anywhere, anywhere, in_vmem, in_smem, in_smem],
        out_specs=(anywhere, in_vmem),
        scratch_shapes=[
            vmem((rows, width), F32),
            vmem((rows, width), F32),
            vmem((rows, width), BF16),
            vmem((rows, width), BF16),
            vmem((H, step, width), BF16),
            vmem((3, H, step, width), BF16),
            vmem((rows, width), F32),
            vmem((rows, width), F32),
            vmem((H, step, width), BF16),
            vmem((H, step, width), BF16),
            vmem((X * ZH, 2, slab, rows), BF16),
            vmem((X * ZH, slab, rows), BF16),
            vmem((ZH, cols, tall, *TILE), BF16),
            vmem((ZH, cols, tall, *TILE), BF16),
            vmem((ZH, cols, tall, *TILE), BF16),
            vmem((ZH, ca, tall, *TILE), F32),
            vmem((ZH, cb, tall, *TILE), F32),
            vmem((ZH, ca, tall, *TILE), BF16),
            vmem((ZH, cb, tall, *TILE), BF16),
            vmem((ZH, cb, tall, *TILE), BF16),
            vmem((ZH, ca, tall, *TILE), BF16),
            vmem((ZH, ca, tall, *TILE), BF16),
            vmem((ZH, cb, tall, *TILE), BF16),
            vmem((ZH, Y * ZL, *TILE), F32),
            vmem((ZH, Y * ZL, *TILE), BF16),
            vmem((ZH, Y - 1, ZL, *TILE), BF16),
            vmem((Z, *TILE), F32),
            vmem((Z, *TILE), BF16),
            vmem((Z - 1, *TILE), BF16),
            vmem((Y * ZL, *TILE), BF16),
            dma((3,)),
            dma((5, H)), dma((3, H)),
            dma((1 + H,)), dma((1 + H,)),
            dma((6, ZH)), dma((6, ZH)),
            dma((ZH, Y - 1)), dma((ZH, Y - 1)),
            dma((Z - 1,)), dma((Z - 1,)),
            dma((ZL - 1,)), dma((ZL - 1,)),
            dma((Y - 1,)), dma((Y - 1,)),
        ],
        compiler_params=pltpu.CompilerParams(
            collective_id=0, has_side_effects=True, vmem_limit_bytes=48 * 1024 * 1024
        ),
        cost_estimate=pl.CostEstimate(
            flops=2 * rows * width * (8 * rows + width), bytes_accessed=10 * rows * width,
            transcendentals=0,
        ),
    )(image_emb, text_emb, pooled, column[:, None], logit_scale, logit_bias)


def solution(mesh):
    in_specs = (
        P(("dp", "tensor"), None),
        P(("dp", "tensor"), None),
        P(("dp", "tensor"), None),
        P(("dp", "tensor")),
        P(),
        P(),
    )
    out_specs = (P(("dp", "tensor"), None), P("tensor", None))
    return jax.shard_map(
        on_device, mesh=mesh, in_specs=in_specs, out_specs=out_specs, check_vma=False
    )
```

time: 551 us -> 106 us (0.19)
  waiting for transfers between devices: 491 us -> 0 us
  Pallas kernels: 0 us -> 96.7 us
  starting transfers between devices: 21.2 us -> 0 us
  between operations: 15.5 us -> 1.95 us
  matrix products: 9.26 us -> 0 us
    psum x1 -> x0, waiting for transfers between devices: 304 us -> none  [on_device(): weight_grad = lax.psum(own_rows, 'dp')]
    unnamed x3 -> x0, waiting for transfers between devices: 164 us -> none
    pallas_call x0 -> x1, Pallas kernels: none -> 96.7 us  [on_device(): pl.pallas_call(kernel, out_shape=(jax.ShapeDtypeStruct((rows, width), F32...]
    ppermute x3 -> x0, waiting for transfers between devices: 23.1 us -> none  [from_behind(): return lax.ppermute(block, axis, route)]
    ppermute x3 -> x0, starting transfers between devices: 21.1 us -> none  [from_behind(): return lax.ppermute(block, axis, route)]
    dot_general x9 -> x0, matrix products: 9.26 us -> none  [the longest x1 3.34 us: on_device(): lax.dot_general(pooled, cached, (((0,), (0,)), ((), ())), preferred_eleme...]
    unnamed x15 -> x8, local copies, waits for them, and re-layouts: 10.9 us -> 5.3 us
  transfers between devices with their start and end apart: 5 -> 0, of which waited for: 5 -> 0; matrix products, arithmetic and copies ran while one was open for 1% -> 0% of each run, Pallas kernels for 0% -> 0%
where the time goes in v1:
time: 106 us; the launch traced here: 105 us
  Pallas kernels  96.7 us (91%)
  local copies, waits for them, and re-layouts  5.44 us (5%)
  between operations  1.95 us (2%)
    pallas_call x1, Pallas kernels, on_device(): pl.pallas_call(kernel, out_shape=(jax.ShapeDtypeStruct((rows, width), F32...  96.7 us
    unnamed x8, local copies, waits for them, and re-layouts  5.3 us

profile of v1, /device:TPU:6, one launch (start us, length us, event | category | flops | bytes accessed | tf_op | source)
XLA Modules:
  0.0 104.8 jit_solution(17076659615327561198)
XLA Ops:
  1.9 0.7 fusion.1
  2.6 0.1 copy.8.column
  2.8 0.0 copy-start
  2.8 1.3 %copy-done = f32[256,1152]{1,0:T(8,128)S(1)} copy-done((f32[256,1152]{1,0:T(8,128)S(1)}, f32[256,1152]{1,0:T(8,128)}, u32[]{:S(2)}) %copy-start) | copy-done | bytes 1179672
  4.1 0.0 copy-start.1
  4.1 1.3 %copy-done.1 = f32[256,1152]{1,0:T(8,128)S(1)} copy-done((f32[256,1152]{1,0:T(8,128)S(1)}, f32[256,1152]{1,0:T(8,128)}, u32[]{:S(2)}) %copy-start.1) | copy-done | bytes 1179672
  5.3 0.0 copy-start.2
  5.3 1.1 %copy-done.2 = bf16[256,1152]{1,0:T(8,128)(2,1)S(1)} copy-done((bf16[256,1152]{1,0:T(8,128)(2,1)S(1)}, bf16[256,1152]{1,0:T(8,128)(2,1)}, u32[]{:S(2)}) %copy-start.2) | copy-done | bytes 589848
  6.4 96.7 %shard_map.77 = (f32[256,1152]{1,0:T(8,128)S(1)}, f32[48,1152]{1,0:T(8,128)S(1)}) custom-call(f32[256,1152]{1,0:T(8,128)S(1)} %copy-done, f32[256,1152]{1,0:T(8,128)S(1)} %copy-done.1, bf16[256,1152]{1,0:T(8,128)(2,1)S(1)} %copy-done.2, s32[256,1]{1,0:T(8,128)S(1)} %copy.8.column, f32[1]{0:T(128)S(6)} %copy.11.scale_ref, f32[1]{0:T(128)S(6)} %copy.12.bias_ref), custom_call_target="tpu_custom_call" | custom-call | flops 1887436800 | bytes 2949120 | tf_op jit(solution)/shard_map/pallas_call | solution.py:412
  103.1 1.0 copy.13
  104.1 0.7 copy.14
Async XLA Ops:
  2.8 1.3 %copy-start = (f32[256,1152]{1,0:T(8,128)S(1)}, f32[256,1152]{1,0:T(8,128)}, u32[]{:S(2)}) copy-start(f32[256,1152]{1,0:T(8,128)} %image_hbm.1) | copy-start | bytes 3538948
  4.1 1.3 %copy-start.1 = (f32[256,1152]{1,0:T(8,128)S(1)}, f32[256,1152]{1,0:T(8,128)}, u32[]{:S(2)}) copy-start(f32[256,1152]{1,0:T(8,128)} %text_hbm.1) | copy-start | bytes 3538948
  5.3 1.1 %copy-start.2 = (bf16[256,1152]{1,0:T(8,128)(2,1)S(1)}, bf16[256,1152]{1,0:T(8,128)(2,1)}, u32[]{:S(2)}) copy-start(bf16[256,1152]{1,0:T(8,128)(2,1)} %pooled_hbm.1) | copy-start | bytes 1769476
